TPU v7x, 32 devices: a whole 2x2x4 slice. The times are simulated.
32 devices in a mesh: row: 4 (over y, core), feat: 8 (over z, x).
Axes of the slice: x: 2, y: 2, z: 4, core: 2. Of those that a mesh axis runs over, the one named last changes fastest.
Arguments:
- table_entries: bfloat16 [4096, 128, 128], P('row', 'feat'), may hold values from -6 to 6
- pseudo_points: bfloat16 [2, 128, 128], replicated, may hold values from -6 to 6
- projection_tensors: bfloat16 [2, 2, 4, 128, 128], replicated, may hold values from -0.5 to 0.5
- expanding_linear: bfloat16 [2, 2, 128, 256], replicated, may hold values from -0.5 to 0.5
- contracting_linear: bfloat16 [2, 2, 256, 128], replicated, may hold values from -0.375 to 0.375
- normalizer_multipliers: float32 [2, 4, 128], replicated, may hold values from 0.1 to 1.9
- sharpness_coefficients: float32 [2, 2, 4], replicated, may hold values from 2 to 12
Outputs:
- embedded: bfloat16 [4096, 128, 128], P(('row', 'feat'))
All inputs are finite; a program needn't handle non-finite values.
Results may differ from a plain program's by a relative error of at most 0.02.
Values may be sent and summed in bfloat16 or wider, within the bound.
A program may use at most 64 MiB of HBM per device.

v0:
```python
import jax
import jax.numpy as jnp
from jax import lax
from jax.sharding import PartitionSpec as P


def layer_norm(values, gain_row):
    values = values.astype(jnp.float32)
    center = values - jnp.mean(values, axis=-1, keepdims=True)
    spread = jnp.mean(center * center, axis=-1, keepdims=True)
    return center * lax.rsqrt(spread + 1e-05) * gain_row


def unit_rms(values):
    return values * lax.rsqrt(jnp.mean(values * values, axis=-1, keepdims=True) + 1e-06)


def partition_channels(values, channel_total):
    return values.reshape(values.shape[0], channel_total, values.shape[1] // channel_total)


def inducing_partials(normed, probe_vectors, key_weight, value_weight, multiplier_list):
    channel_total = multiplier_list.shape[0]
    head_width = probe_vectors.shape[1] // channel_total
    lookup_vectors = unit_rms(
        jnp.dot(normed, key_weight, preferred_element_type=jnp.float32)
    ).astype(jnp.bfloat16)
    value_matrix_rows = jnp.dot(normed, value_weight, preferred_element_type=jnp.float32).astype(
        jnp.bfloat16
    )
    affinity_logits = jnp.einsum(
        "ljc,ejc->jle",
        partition_channels(probe_vectors, channel_total),
        partition_channels(lookup_vectors, channel_total),
        preferred_element_type=jnp.float32,
    )
    softmax_weights = jnp.exp(affinity_logits * (multiplier_list / head_width)[:, None, None])
    totals = jnp.sum(softmax_weights, axis=2)
    weighted_values = jnp.einsum(
        "qab,bqg->aqg",
        softmax_weights.astype(jnp.bfloat16),
        partition_channels(value_matrix_rows, channel_total),
        preferred_element_type=jnp.float32,
    )
    return (totals, weighted_values.reshape(probe_vectors.shape[0], probe_vectors.shape[1]))


def inducing_finish(
    totals,
    weighted_values,
    anchor,
    out_weight,
    up_weight,
    down_weight,
    gain_mlp,
    gain_keys,
    key_weight,
    value_weight,
):
    channel_total = totals.shape[0]
    query_count = weighted_values.shape[0]
    blended = (
        weighted_values.reshape(query_count, channel_total, -1) / jnp.transpose(totals)[:, :, None]
    )
    blended = blended.reshape(query_count, -1).astype(jnp.bfloat16)
    summary = anchor.astype(jnp.float32) + jnp.dot(
        blended, out_weight, preferred_element_type=jnp.float32
    )
    hidden = jax.nn.gelu(
        jnp.dot(
            layer_norm(summary, gain_mlp).astype(jnp.bfloat16),
            up_weight,
            preferred_element_type=jnp.float32,
        ),
        approximate=True,
    ).astype(jnp.bfloat16)
    refined = summary + jnp.dot(hidden, down_weight, preferred_element_type=jnp.float32)
    normed = layer_norm(refined, gain_keys).astype(jnp.bfloat16)
    lookup_vectors = unit_rms(
        jnp.dot(normed, key_weight, preferred_element_type=jnp.float32)
    ).astype(jnp.bfloat16)
    value_matrix_rows = jnp.dot(normed, value_weight, preferred_element_type=jnp.float32).astype(
        jnp.bfloat16
    )
    return (lookup_vectors, value_matrix_rows)


def row_side(
    current,
    normed,
    lookup_vectors,
    value_matrix_rows,
    query_weight,
    out_weight,
    up_weight,
    down_weight,
    gain_mlp,
    multiplier_list,
):
    channel_total = multiplier_list.shape[0]
    head_width = lookup_vectors.shape[1] // channel_total
    probe_vectors = unit_rms(
        jnp.dot(normed, query_weight, preferred_element_type=jnp.float32)
    ).astype(jnp.bfloat16)
    affinity_logits = jnp.einsum(
        "lgu,bgu->lgb",
        partition_channels(probe_vectors, channel_total),
        partition_channels(lookup_vectors, channel_total),
        preferred_element_type=jnp.float32,
    )
    softmax_weights = jnp.exp(affinity_logits * (multiplier_list / head_width)[None, :, None])
    softmax_weights = (softmax_weights / jnp.sum(softmax_weights, axis=2, keepdims=True)).astype(
        jnp.bfloat16
    )
    attended_rows = jnp.einsum(
        "gql,lqv->gqv",
        softmax_weights,
        partition_channels(value_matrix_rows, channel_total),
        preferred_element_type=jnp.float32,
    )
    attended_rows = attended_rows.reshape(current.shape[0], -1).astype(jnp.bfloat16)
    updated = current.astype(jnp.float32) + jnp.dot(
        attended_rows, out_weight, preferred_element_type=jnp.float32
    )
    hidden = jax.nn.gelu(
        jnp.dot(
            layer_norm(updated, gain_mlp).astype(jnp.bfloat16),
            up_weight,
            preferred_element_type=jnp.float32,
        ),
        approximate=True,
    ).astype(jnp.bfloat16)
    updated = updated + jnp.dot(hidden, down_weight, preferred_element_type=jnp.float32)
    return updated.astype(jnp.bfloat16)


def body(
    table_entries,
    pseudo_points,
    projection_tensors,
    expanding_linear,
    contracting_linear,
    normalizer_multipliers,
    sharpness_coefficients,
):
    current = jnp.swapaxes(table_entries, 0, 1)
    layers = normalizer_multipliers.shape[0]
    for stack_position in range(layers):
        gain_rows = normalizer_multipliers[stack_position]
        multiplier_list = sharpness_coefficients[stack_position]
        weights_ind = projection_tensors[stack_position, 0]
        weights_row = projection_tensors[stack_position, 1]
        normed = layer_norm(current, gain_rows[0]).astype(jnp.bfloat16)
        probe_vectors = unit_rms(
            jnp.dot(
                pseudo_points[stack_position], weights_ind[0], preferred_element_type=jnp.float32
            )
        ).astype(jnp.bfloat16)
        totals, weighted_values = lax.map(
            lambda column: inducing_partials(
                column, probe_vectors, weights_ind[1], weights_ind[2], multiplier_list[0]
            ),
            normed,
        )

        def finish_terms(partial_pair):
            return inducing_finish(
                partial_pair[0],
                partial_pair[1],
                pseudo_points[stack_position],
                weights_ind[3],
                expanding_linear[stack_position, 0],
                contracting_linear[stack_position, 0],
                gain_rows[2],
                gain_rows[1],
                weights_row[1],
                weights_row[2],
            )

        totals, weighted_values = (
            lax.psum(totals.astype(jnp.bfloat16), "row").astype(jnp.float32),
            lax.psum(weighted_values.astype(jnp.bfloat16), "row").astype(jnp.float32),
        )
        lookup_vectors, value_matrix_rows = lax.map(finish_terms, (totals, weighted_values))

        def row_terms(bundle):
            return row_side(
                bundle[0],
                bundle[1],
                bundle[2],
                bundle[3],
                weights_row[0],
                weights_row[3],
                expanding_linear[stack_position, 1],
                contracting_linear[stack_position, 1],
                gain_rows[3],
                multiplier_list[1],
            )

        if stack_position + 1 < layers:
            current = lax.map(row_terms, (current, normed, lookup_vectors, value_matrix_rows))
    current = lax.map(row_terms, (current, normed, lookup_vectors, value_matrix_rows))
    return lax.all_to_all(
        jnp.swapaxes(current, 0, 1), "feat", split_axis=0, concat_axis=1, tiled=True
    )


def solution(mesh):
    return jax.shard_map(
        body,
        mesh=mesh,
        in_specs=(P("row", "feat", None), P(), P(), P(), P(), P(), P()),
        out_specs=P(("row", "feat"), None, None),
        check_vma=False,
    )
```

profile of v0, /device:TPU:0, one launch (start us, length us, event | category | flops | bytes accessed | tf_op | source)
XLA Modules:
  0.0 665.3 jit_solution(18116324749532174247)
XLA Ops:
  6.6 4.6 convert_reduce_fusion.1
  11.2 5.3 fusion.207
  16.9 8.7 %fusion.209 = bf16[16,1024,128]{2,1,0:T(8,128)(2,1)} fusion(f32[128]{0:T(128)S(1)} %get-tuple-element.612, f32[16,1024]{1,0:T(8,128)S(1)} %add_rsqrt_fusion.13, f32[16,1024]{1,0:T(8,128)S(1)} %broadcast_multiply_fusion.7, bf16[16,1024,128]{2,0,1:T(8,128)(2,1)} %bitcast.496), kind=kLoop, calls=%fused_computation.277 | loop fusion | flops 10485760 | bytes 8520192 | tf_op jit(solution)/shard_map/convert_element_type | solution.py:153
  25.8 60.5 %while.68 = (s32[]{:T(128)}, bf16[16,4,128]{2,1,0:T(4,128)(2,1)S(1)}, bf16[16,128,128]{1,2,0:T(8,128)(2,1)S(1)}, bf16[16,1024,128]{2,1,0:T(8,128)(2,1)}, bf16[4,...) while((s32[]{:T(128)}, ...), condition=%wide.region_6.7_spmd, body=%wide.region_3.6_spmd.sunk | while | flops 136970752 | bytes 7032989 | solution.py:159
  87.5 6.6 copy.50
  94.2 12.7 %psum.29 = bf16[16,4,128]{2,1,0:T(4,128)(2,1)S(1)} all-reduce(bf16[16,4,128]{2,1,0:T(4,128)(2,1)S(1)} %get-tuple-element.312), channel_id=1, replica_groups=mesh['row'=4,'feat'=8] {'row'}, use_global_device_ids=true, to_apply=%region_7.8 | all-reduce | flops 8192 | bytes 32768 | tf_op jit(solution)/shard_map/psum | solution.py:181
  106.9 16.2 %all-reduce.3.cloned.1.call-done = bf16[16,128,128]{1,2,0:T(8,128)(2,1)} async-done(((bf16[16,128,128]{1,2,0:T(8,128)(2,1)}), bf16[16,128,128]{1,2,0:T(8,128)(2,1)}) %all-reduce.3.cloned.1.call-update) | async-done | bytes 524304 | tf_op jit(solution)/shard_map/psum | solution.py:182
  124.5 36.4 %while.69 = (s32[]{:T(128)}, bf16[16,128,128]{1,2,0:T(8,128)(2,1)S(1)}, bf16[16,128,128]{2,1,0:T(8,128)(2,1)S(1)}, bf16[2,128,128]{1,2,0:T(8,128)(2,1)S(1)}, f32...) while((s32[]{:T(128)}, ...), condition=%wide.region_15.16_spmd, body=%wide.region_9.15_spmd.sunk | while | flops 30146944 | bytes 1136261 | solution.py:184
  160.9 2.5 broadcast.394.clone
  163.4 115.5 %while.70 = (s32[]{:T(128)}, bf16[16,1024,128]{1,2,0:T(8,128)(2,1)}, bf16[16,1024,128]{1,2,0:T(8,128)(2,1)}, bf16[16,128,128]{2,1,0:T(8,128)(2,1)S(1)}, bf16[16,...) while((s32[]{:T(128)}, ...), condition=%wide.region_21.22_spmd, body=%wide.region_16.21_spmd.sunk | while | flops 275642368 | bytes 13916921 | solution.py:201
  168.3 2.3 fusion.309
  175.5 2.3 fusion.309
  177.8 1.4 multiply_reduce_fusion.30
  182.7 2.3 fusion.309
  185.0 1.4 multiply_reduce_fusion.30
  190.0 2.3 fusion.309
  192.3 1.4 multiply_reduce_fusion.30
  197.2 2.3 fusion.309
  199.5 1.4 multiply_reduce_fusion.30
  204.4 2.3 fusion.309
  206.7 1.4 multiply_reduce_fusion.30
  211.6 2.3 fusion.309
  218.9 2.3 fusion.309
  226.1 2.3 fusion.309
  233.3 2.3 fusion.309
  240.5 2.3 fusion.309
  242.8 1.4 multiply_reduce_fusion.30
  247.8 2.3 fusion.309
  250.1 1.4 multiply_reduce_fusion.30
  255.0 2.3 fusion.309
  262.2 2.3 fusion.309
  269.4 2.3 fusion.309
  271.7 1.4 multiply_reduce_fusion.30
  276.6 2.3 fusion.309
  278.9 6.4 copy.55
  285.3 3.5 convert_reduce_fusion
  288.9 4.8 fusion.204
  293.7 6.3 fusion.206
  300.1 60.5 %while.71 = (s32[]{:T(128)}, bf16[16,4,128]{2,1,0:T(4,128)(2,1)S(1)}, bf16[16,128,128]{1,2,0:T(8,128)(2,1)S(1)}, bf16[16,1024,128]{2,1,0:T(8,128)(2,1)}, bf16[4,...) while((s32[]{:T(128)}, ...), condition=%wide.region_28.29_spmd, body=%wide.region_25.28_spmd.sunk | while | flops 136970752 | bytes 7032989 | solution.py:159
  361.4 10.5 %psum.31 = bf16[16,4,128]{2,1,0:T(4,128)(2,1)S(1)} all-reduce(bf16[16,4,128]{2,1,0:T(4,128)(2,1)S(1)} %get-tuple-element.317), channel_id=1, replica_groups=mesh['row'=4,'feat'=8] {'row'}, use_global_device_ids=true, to_apply=%region_29.30 | all-reduce | flops 8192 | bytes 32768 | tf_op jit(solution)/shard_map/psum | solution.py:181
  371.9 22.8 %all-reduce.5.cloned.1.call-done = bf16[16,128,128]{1,2,0:T(8,128)(2,1)} async-done(((bf16[16,128,128]{1,2,0:T(8,128)(2,1)}), bf16[16,128,128]{1,2,0:T(8,128)(2,1)}) %all-reduce.5.cloned.1.call-update) | async-done | bytes 524304 | tf_op jit(solution)/shard_map/psum | solution.py:182
  396.0 36.4 %while.72 = (s32[]{:T(128)}, bf16[16,128,128]{1,2,0:T(8,128)(2,1)S(1)}, bf16[16,128,128]{2,1,0:T(8,128)(2,1)S(1)}, bf16[2,128,128]{1,2,0:T(8,128)(2,1)S(1)}, f32...) while((s32[]{:T(128)}, ...), condition=%wide.region_37.38_spmd, body=%wide.region_31.37_spmd.sunk | while | flops 30146944 | bytes 1136261 | solution.py:184
  432.4 2.5 broadcast.394
  435.0 115.5 %while.73 = (s32[]{:T(128)}, bf16[16,1024,128]{1,2,0:T(8,128)(2,1)}, bf16[16,1024,128]{1,2,0:T(8,128)(2,1)}, bf16[16,128,128]{2,1,0:T(8,128)(2,1)S(1)}, bf16[16,...) while((s32[]{:T(128)}, ...), condition=%wide.region_43.44_spmd, body=%wide.region_38.43_spmd.sunk | while | flops 275642368 | bytes 13916921 | solution.py:202
  439.9 2.3 fusion.331
  442.2 1.4 multiply_reduce_fusion.36
  447.1 2.3 fusion.331
  454.3 2.3 fusion.331
  461.5 2.3 fusion.331
  468.8 2.3 fusion.331
  476.0 2.3 fusion.331
  483.2 2.3 fusion.331
  490.4 2.3 fusion.331
  497.6 2.3 fusion.331
  504.8 2.3 fusion.331
  512.1 2.3 fusion.331
  519.3 2.3 fusion.331
  526.5 2.3 fusion.331
  533.7 2.3 fusion.331
  540.9 2.3 fusion.331
  548.1 2.3 fusion.331
  550.4 6.8 %copy.59 = bf16[16,1024,128]{2,0,1:T(8,128)(2,1)} copy(bf16[16,1024,128]{1,2,0:T(8,128)(2,1)} %get-tuple-element.320) | data formatting | bytes 8388608 | tf_op jit(solution)/shard_map/while | solution.py:202
  557.3 98.0 %all_to_all.18 = bf16[1024,16,128]{2,1,0:T(8,128)(2,1)S(1)} all-to-all(bf16[1024,16,128]{2,1,0:T(8,128)(2,1)} %bitcast.504), channel_id=1, replica_groups=mesh['row'=4,'feat'=8] {'feat'}, dimensions={0} | all-to-all | bytes 8388608 | tf_op jit(solution)/shard_map/all_to_all | solution.py:203
  655.2 3.3 copy.60
  (1384 shorter events, 336.8 us)
Async XLA Ops:
  6.5 116.6 %all-reduce.3.cloned.1.call-start = ((), (), s32[]{:S(2)}) async-start(), calls=%async_computation.1 | async-start | bytes 1048576 | tf_op jit(solution)/shard_map/psum | solution.py:182
  6.5 4.7 copy-start
  6.5 10.0 %copy-start.10 = (f32[2,4,128]{2,1,0:T(4,128)S(1)}, f32[2,4,128]{2,1,0:T(4,128)}, u32[]{:S(2)}) copy-start(f32[2,4,128]{2,1,0:T(4,128)} %param.24) | copy-start | bytes 12292
  6.5 10.0 %copy-start.8 = (bf16[2,2,4,128,128]{4,3,2,1,0:T(8,128)(2,1)S(1)}, bf16[2,2,4,128,128]{4,3,2,1,0:T(8,128)(2,1)}, u32[]{:S(2)}) copy-start(bf16[2,2,4,128,128]{4,3,2,1,0:T(8,128)(2,1)} %param.21) | copy-start | bytes 1572868
  6.5 10.1 %copy-start.9 = (bf16[2,128,128]{2,1,0:T(8,128)(2,1)S(1)}, bf16[2,128,128]{2,1,0:T(8,128)(2,1)}, u32[]{:S(2)}) copy-start(bf16[2,128,128]{2,1,0:T(8,128)(2,1)} %param.20) | copy-start | bytes 196612
  6.5 10.3 %copy-start.11 = (f32[2,2,4]{2,1,0:T(2,128)S(1)}, f32[2,2,4]{2,1,0:T(2,128)}, u32[]{:S(2)}) copy-start(f32[2,2,4]{2,1,0:T(2,128)} %param.25) | copy-start | bytes 196
  87.1 307.6 %all-reduce.5.cloned.1.call-start = ((), (), s32[]{:S(2)}) async-start(), calls=%async_computation.2 | async-start | bytes 1048576 | tf_op jit(solution)/shard_map/psum | solution.py:182
  87.5 37.0 %copy-start.12 = (bf16[2,2,128,256]{3,2,1,0:T(8,128)(2,1)S(1)}, bf16[2,2,128,256]{3,2,1,0:T(8,128)(2,1)}, u32[]{:S(2)}) copy-start(bf16[2,2,128,256]{3,2,1,0:T(8,128)(2,1)} %param.22) | copy-start | bytes 786436
  166.9 3.7 copy-start.5
  170.6 1.5 copy-start.4
  174.1 3.7 copy-start.5
  177.8 1.5 copy-start.4
  181.3 3.7 copy-start.5
  185.0 1.5 copy-start.4
  188.5 3.7 copy-start.5
  192.3 1.5 copy-start.4
  195.8 3.7 copy-start.5
  199.5 1.5 copy-start.4
  203.0 3.7 copy-start.5
  206.7 1.5 copy-start.4
  210.2 3.7 copy-start.5
  213.9 1.5 copy-start.4
  217.4 3.7 copy-start.5
  221.2 1.5 copy-start.4
  224.7 3.7 copy-start.5
  228.4 1.5 copy-start.4
  231.9 3.7 copy-start.5
  235.6 1.5 copy-start.4
  239.1 3.7 copy-start.5
  242.8 1.5 copy-start.4
  246.3 3.7 copy-start.5
  250.1 1.5 copy-start.4
  253.6 3.7 copy-start.5
  257.3 1.5 copy-start.4
  260.8 3.7 copy-start.5
  264.5 1.5 copy-start.4
  268.0 3.7 copy-start.5
  271.7 1.5 copy-start.4
  275.2 3.7 copy-start.5
  285.3 3.5 copy-start.1
  435.0 1.5 copy-start.6
  438.5 3.7 copy-start.7
  442.2 1.5 copy-start.6
  445.7 3.7 copy-start.7
  449.4 1.5 copy-start.6
  452.9 3.7 copy-start.7
  456.6 1.5 copy-start.6
  460.1 3.7 copy-start.7
  463.8 1.5 copy-start.6
  467.3 3.7 copy-start.7
  471.0 1.5 copy-start.6
  474.5 3.7 copy-start.7
  478.3 1.5 copy-start.6
  481.8 3.7 copy-start.7
  485.5 1.5 copy-start.6
  489.0 3.7 copy-start.7
  496.2 3.7 copy-start.7
  503.4 3.7 copy-start.7
  510.6 3.7 copy-start.7
  517.8 3.7 copy-start.7
  525.1 3.7 copy-start.7
  532.3 3.7 copy-start.7
  539.5 3.7 copy-start.7
  546.7 3.7 copy-start.7
  (11 other events, 14.9 us)
Sparse Core Ops, SparseCore 0:
  87.2 35.8 all-reduce.2
  361.5 33.0 all-reduce.4
where the time goes:
time: 675 us; the launch traced here: 665 us
  matrix products  377 us (56%)
  blocking collectives  121 us (18%)
  local copies, waits for them, and re-layouts  61.3 us (9%)
  other arithmetic  46 us (7%)
  waiting for transfers between devices  39 us (6%)
  between operations  13.7 us (2%)
  loops' own time  7.25 us (1%)
    all_to_all x1, blocking collectives, body(): lax.all_to_all(jnp.swapaxes(current, 0, 1), 'feat', split_axis=0, concat_...  98 us
    dot_general x32, matrix products, row_side(): jnp.dot(hidden, down_weight, preferred_element_type=jnp.float32)  73.4 us
    dot_general x32, matrix products, row_side(): jnp.dot(normed, query_weight, preferred_element_type=jnp.float32)  44.5 us
    dot_general x32, matrix products, inducing_finish(): jnp.dot(hidden, down_weight, preferred_element_type=jnp.float32)  41.5 us
    dot_general x32, matrix products, row_side(): jnp.dot(attended_rows, out_weight, preferred_element_type=jnp.float32)  41.1 us
    dot_general x32, matrix products, inducing_partials(): jnp.dot(normed, key_weight, preferred_element_type=jnp.float32)  39.3 us
    psum x2, waiting for transfers between devices, body(): lax.psum(weighted_values.astype(jnp.bfloat16), 'row').astype(jnp.float32)  39 us
    dot_general x32, matrix products, inducing_partials(): jnp.dot(normed, value_weight, preferred_element_type=jnp.float32)  38.9 us
  transfers between devices with their start and end apart: 2, of which 2 were waited for; matrix products, arithmetic and copies ran while one was open for 1% of the time, Pallas kernels for 0%

commit v1 on v0

v1 whole, which is shorter than its diff:
```python
import functools
import math

import jax
import jax.numpy as jnp
from jax import lax
from jax.experimental import pallas as pl
from jax.experimental.pallas import tpu as pltpu
from jax.sharding import PartitionSpec as P

GROUP = 2
CHUNK = 512
MESH = pl.DeviceIdType.MESH
F32, BF16 = jnp.float32, jnp.bfloat16


def dot(a, b):
    return jnp.dot(a, b, preferred_element_type=F32)


def dot_nt(a, b):
    return lax.dot_general(a, b, (((1,), (1,)), ((), ())), preferred_element_type=F32)


def dot_tn(a, b):
    return lax.dot_general(a, b, (((0,), (0,)), ((), ())), preferred_element_type=F32)


def layer_norm(values, gain_row):
    center = values - jnp.mean(values, axis=-1, keepdims=True)
    spread = jnp.mean(center * center, axis=-1, keepdims=True)
    return (center * lax.rsqrt(spread + 1e-05) * gain_row).astype(BF16)


def unit_rms(values):
    return values * lax.rsqrt(jnp.mean(values * values, axis=-1, keepdims=True) + 1e-06)


def gelu(x):
    c = math.sqrt(2.0 / math.pi)
    return (0.5 * x) * (1.0 + jnp.tanh(x * (c + (c * 0.044715) * (x * x))))


def kernel(
    heads,
    x_ref,
    points_ref,
    proj_ref,
    up_ref,
    down_ref,
    gain_ref,
    sharp_ref,
    out_ref,
    state,
    final,
    queries,
    probes,
    wkvq,
    wkv2,
    weights_t,
    values_aug,
    keys_bd,
    values_bd,
    part,
    row_send,
    row_recv,
    out_send,
    out_recv,
    own_sem,
):
    layers = points_ref.shape[0]
    m, e = points_ref.shape[1], points_ref.shape[2]
    cols, rows = x_ref.shape[0], x_ref.shape[1]
    nrow, nfeat = part.shape[2], out_recv.shape[1]
    groups = cols // GROUP
    block = rows // nfeat
    width = e // heads
    me_r, me_f = lax.axis_index("row"), lax.axis_index("feat")

    def row_peer(d):
        return (lax.rem(me_r + d, nrow), me_f)

    def feat_peer(d):
        return (me_r, lax.rem(me_f + d, nfeat))

    barrier = pltpu.get_barrier_semaphore()
    for d in range(1, nrow):
        pl.semaphore_signal(barrier, inc=1, device_id=row_peer(d), device_id_type=MESH)
    for d in range(1, nfeat):
        pl.semaphore_signal(barrier, inc=1, device_id=feat_peer(d), device_id_type=MESH)

    def lane_head(shape):
        return lax.broadcasted_iota(jnp.int32, shape, 1) // width

    def head_mask(h, shape):
        return lane_head(shape) == h

    def lane_scale(b, side):
        lanes = lane_head((1, e))
        scale = jnp.zeros((1, e), F32)
        for h in range(heads):
            scale = jnp.where(lanes == h, sharp_ref[b, side, h], scale)
        return scale * (math.log2(math.e) / width)

    for b in range(layers):
        for at, (side, which) in enumerate(((0, 1), (0, 2), (1, 0))):
            wkvq[b, :, at * e : (at + 1) * e] = proj_ref[b, side, which]
        for at, (side, which) in enumerate(((1, 1), (1, 2))):
            wkv2[b, :, at * e : (at + 1) * e] = proj_ref[b, side, which]
        probe = unit_rms(dot(points_ref[b], proj_ref[b, 0, 0])) * lane_scale(b, 0)
        for h in range(heads):
            probes[b, h * m : (h + 1) * m, :] = jnp.where(
                head_mask(h, (m, e)), probe, 0.0
            ).astype(BF16)
    for g in range(GROUP):
        for h in range(heads):
            values_bd[g, h * m : (h + 1) * m, e:] = head_mask(h, (m, e)).astype(F32).astype(BF16)
    values_aug[:, e:] = jnp.ones((values_aug.shape[0], e), BF16)
    select_row = lax.broadcasted_iota(jnp.int32, (16, e), 0)
    select_lane = lax.broadcasted_iota(jnp.int32, (16, e), 1)
    select = (select_lane == select_row * width).astype(F32).astype(BF16)
    spread = (select_lane // width == select_row).astype(F32).astype(BF16)

    pl.semaphore_wait(barrier, nrow - 1 + nfeat - 1)

    def by_head(stacked):
        total = stacked[:m]
        for h in range(1, heads):
            total = jnp.where(head_mask(h, (m, e)), stacked[h * m : (h + 1) * m], total)
        return total

    def partial_chunk(b, c, at, current):
        normed = layer_norm(current, gain_ref[b, 0][None, :])
        mixed = dot(normed, wkvq[b])
        keys = unit_rms(mixed[:, :e]).astype(BF16)
        values_aug[:, :e] = mixed[:, e : 2 * e].astype(BF16)
        queries[c, pl.ds(at, CHUNK), :] = unit_rms(mixed[:, 2 * e :]).astype(BF16)
        weights_t[...] = jnp.exp2(dot_nt(probes[b], keys)).astype(BF16)
        stacked = dot(weights_t[...], values_aug[...])
        return by_head(stacked[:, :e]), by_head(stacked[:, e:])

    def row_copy(b, t, d):
        return pltpu.make_async_remote_copy(
            src_ref=part.at[b, t, 0],
            dst_ref=part.at[b, t, d],
            send_sem=row_send.at[b, t, d],
            recv_sem=row_recv.at[b, t, d],
            device_id=row_peer(d),
            device_id_type=MESH,
        )

    def send_partials(b, t, g, weighted, totals):
        part[b, t, 0, g, :m, :] = weighted.astype(BF16)
        part[b, t, 0, g, m:, :] = dot_nt(select, totals.astype(BF16)).astype(BF16)

    def finish(b, t):
        for d in range(1, nrow):
            copy = row_copy(b, t, d)
            copy.wait_send()
            copy.wait_recv()
        blended = []
        for g in range(GROUP):
            total = part[b, t, 0, g].astype(F32)
            for d in range(1, nrow):
                total = total + part[b, t, d, g].astype(F32)
            inverse = 1.0 / jnp.where(select_row < heads, total[m:], 1.0)
            high = inverse.astype(BF16)
            low = (inverse - high.astype(F32)).astype(BF16)
            scale = dot_tn(high, spread) + dot_tn(low, spread)
            blended.append((total[:m] * scale).astype(BF16))
        blended = jnp.concatenate(blended, axis=0)
        anchor = jnp.concatenate([points_ref[b].astype(F32)] * GROUP, axis=0)
        summary = anchor + dot(blended, proj_ref[b, 0, 3])
        hidden = gelu(dot(layer_norm(summary, gain_ref[b, 2][None, :]), up_ref[b, 0])).astype(BF16)
        refined = summary + dot(hidden, down_ref[b, 0])
        normed = layer_norm(refined, gain_ref[b, 1][None, :])
        mixed = dot(normed, wkv2[b])
        keys = unit_rms(mixed[:, :e]) * lane_scale(b, 1)
        for g in range(GROUP):
            key = keys[g * m : (g + 1) * m]
            value = mixed[g * m : (g + 1) * m, e:]
            for h in range(heads):
                mask = head_mask(h, (m, e))
                keys_bd[g, h * m : (h + 1) * m, :] = jnp.where(mask, key, 0.0).astype(BF16)
                values_bd[g, h * m : (h + 1) * m, :e] = jnp.where(mask, value, 0.0).astype(BF16)

    def row_chunk(b, g, c, at, current):
        weights = jnp.exp2(dot_nt(queries[c, pl.ds(at, CHUNK), :], keys_bd[g])).astype(BF16)
        both = dot(weights, values_bd[g])
        attended = (both[:, :e] / both[:, e:]).astype(BF16)
        updated = current + dot(attended, proj_ref[b, 1, 3])
        hidden = gelu(dot(layer_norm(updated, gain_ref[b, 3][None, :]), up_ref[b, 1])).astype(BF16)
        return (updated + dot(hidden, down_ref[b, 1])).astype(BF16)

    chunks = rows // CHUNK

    def stage(b, t):
        if b > 0:
            finish(b - 1, t)

        def column(g, carry):
            c = t * GROUP + g
            source = x_ref if b <= 1 else state

            def step(i, sums):
                at = pl.multiple_of(i * CHUNK, CHUNK)
                current = source[c, pl.ds(at, CHUNK), :].astype(F32)
                if b > 0:
                    new = row_chunk(b - 1, g, c, at, current)
                    if b == layers:
                        final[c, pl.ds(at, CHUNK), :] = new
                        return sums
                    state[c, pl.ds(at, CHUNK), :] = new
                    current = new.astype(F32)
                weighted, totals = partial_chunk(b, c, at, current)
                return sums[0] + weighted, sums[1] + totals

            if b == layers:
                lax.fori_loop(0, chunks, step, 0)
            else:
                zero = jnp.zeros((m, e), F32)
                weighted, totals = lax.fori_loop(0, chunks, step, (zero, zero))
                send_partials(b, t, g, weighted, totals)
            return carry

        lax.fori_loop(0, GROUP, column, 0)
        if b < layers:
            for d in range(1, nrow):
                row_copy(b, t, d).start()
        else:
            for d in range(1, nfeat):
                out_copy(t, d).start()
            own_copy(t).start()

    def out_copy(t, d):
        k = lax.rem(me_f + d, nfeat)
        return pltpu.make_async_remote_copy(
            src_ref=final.at[pl.ds(t * GROUP, GROUP), pl.ds(k * block, block)],
            dst_ref=out_ref.at[pl.ds(me_f * cols + t * GROUP, GROUP)],
            send_sem=out_send.at[t, d],
            recv_sem=out_recv.at[t, d],
            device_id=feat_peer(d),
            device_id_type=MESH,
        )

    def own_copy(t):
        return pltpu.make_async_copy(
            final.at[pl.ds(t * GROUP, GROUP), pl.ds(me_f * block, block)],
            out_ref.at[pl.ds(me_f * cols + t * GROUP, GROUP)],
            own_sem.at[t],
        )

    def turn(s, carry):
        for b in range(layers + 1):
            t = s - b

            @pl.when(jnp.logical_and(t >= 0, t < groups))
            def _():
                stage(b, t)

        return carry

    lax.fori_loop(0, groups + layers, turn, 0)

    def drain(t, carry):
        for d in range(1, nfeat):
            out_copy(t, d).wait_send()
            source = lax.rem(me_f + nfeat - d, nfeat)
            pltpu.make_async_remote_copy(
                src_ref=final.at[pl.ds(t * GROUP, GROUP), pl.ds(me_f * block, block)],
                dst_ref=out_ref.at[pl.ds(source * cols + t * GROUP, GROUP)],
                send_sem=out_send.at[t, d],
                recv_sem=out_recv.at[t, d],
                device_id=feat_peer(d),
                device_id_type=MESH,
            ).wait_recv()
        own_copy(t).wait()
        return carry

    lax.fori_loop(0, groups, drain, 0)


def body(
    table_entries,
    pseudo_points,
    projection_tensors,
    expanding_linear,
    contracting_linear,
    normalizer_multipliers,
    sharpness_coefficients,
    *,
    nrow,
    nfeat,
):
    rows, cols, e = table_entries.shape
    layers, m = pseudo_points.shape[:2]
    heads = sharpness_coefficients.shape[2]
    groups = cols // GROUP
    vmem = pl.BlockSpec(memory_space=pltpu.VMEM)
    columns = pl.pallas_call(
        functools.partial(kernel, heads),
        out_shape=jax.ShapeDtypeStruct((cols * nfeat, rows // nfeat, e), BF16),
        in_specs=[vmem] * 6 + [pl.BlockSpec(memory_space=pltpu.SMEM)],
        out_specs=pl.BlockSpec(memory_space=pl.ANY),
        scratch_shapes=[
            pltpu.VMEM((cols, rows, e), BF16),
            pltpu.VMEM((cols, rows, e), BF16),
            pltpu.VMEM((cols, rows, e), BF16),
            pltpu.VMEM((layers, heads * m, e), BF16),
            pltpu.VMEM((layers, e, 3 * e), BF16),
            pltpu.VMEM((layers, e, 2 * e), BF16),
            pltpu.VMEM((heads * m, CHUNK), BF16),
            pltpu.VMEM((CHUNK, 2 * e), BF16),
            pltpu.VMEM((GROUP, heads * m, e), BF16),
            pltpu.VMEM((GROUP, heads * m, 2 * e), BF16),
            pltpu.VMEM((layers, groups, nrow, GROUP, m + 16, e), BF16),
            pltpu.SemaphoreType.DMA((layers, groups, nrow)),
            pltpu.SemaphoreType.DMA((layers, groups, nrow)),
            pltpu.SemaphoreType.DMA((groups, nfeat)),
            pltpu.SemaphoreType.DMA((groups, nfeat)),
            pltpu.SemaphoreType.DMA((groups,)),
        ],
        compiler_params=pltpu.CompilerParams(
            collective_id=0, has_side_effects=True, vmem_limit_bytes=56 * 2**20
        ),
    )(
        jnp.swapaxes(table_entries, 0, 1),
        pseudo_points,
        projection_tensors,
        expanding_linear,
        contracting_linear,
        normalizer_multipliers,
        sharpness_coefficients,
    )
    return jnp.swapaxes(columns, 0, 1)


def solution(mesh):
    return jax.shard_map(
        functools.partial(body, nrow=mesh.shape["row"], nfeat=mesh.shape["feat"]),
        mesh=mesh,
        in_specs=(P("row", "feat", None), P(), P(), P(), P(), P(), P()),
        out_specs=P(("row", "feat"), None, None),
        check_vma=False,
    )
```

time: 675 us -> 209 us (0.31); the launches traced: 665 us -> 207 us
  matrix products: 377 us -> 0 us
  Pallas kernels: 0 us -> 195 us
  blocking collectives: 121 us -> 0 us
  local copies, waits for them, and re-layouts: 61.3 us -> 12.2 us
  other arithmetic: 46 us -> 0 us
  waiting for transfers between devices: 39 us -> 0 us
  between operations: 13.7 us -> 0.01 us
  loops' own time: 7.25 us -> 0 us
    dot_general x418 -> x0, matrix products: 377 us -> none  [the longest x32 73.4 us: row_side(): jnp.dot(hidden, down_weight, preferred_element_type=jnp.float32)]
    pallas_call x0 -> x1, Pallas kernels: none -> 195 us  [body(): pl.pallas_call(functools.partial(kernel, heads), out_shape=jax.ShapeDtype...]
    all_to_all x1 -> x0, blocking collectives: 98 us -> none  [body(): lax.all_to_all(jnp.swapaxes(current, 0, 1), 'feat', split_axis=0, concat_...]
    psum x2 -> x0, waiting for transfers between devices: 39 us -> none  [body(): lax.psum(weighted_values.astype(jnp.bfloat16), 'row').astype(jnp.float32)]
    dynamic_slice x96 -> x0, local copies, waits for them, and re-layouts: 28.5 us -> none  [body(): lax.map(row_terms, (current, normed, lookup_vectors, value_matrix_rows))]
    psum x2 -> x0, blocking collectives: 23.2 us -> none  [body(): lax.psum(totals.astype(jnp.bfloat16), 'row').astype(jnp.float32)]
    reduce_sum x100 -> x0, other arithmetic: 22.8 us -> none  [the longest x98 14.7 us: layer_norm(): spread = jnp.mean(center * center, axis=-1, keepdims=True)]
    convert_element_type x104 -> x0, other arithmetic: 20.4 us -> none  [the longest x2 15.1 us: body(): normed = layer_norm(current, gain_rows[0]).astype(jnp.bfloat16)]
  transfers between devices with their start and end apart: 2 -> 0, of which waited for: 2 -> 0; matrix products, arithmetic and copies ran while one was open for 1% -> 0% of each run, Pallas kernels for 0% -> 0%
where the time goes in v1:
time: 209 us; the launch traced here: 207 us
  Pallas kernels  195 us (93%)
  local copies, waits for them, and re-layouts  12.2 us (6%)
    pallas_call x1, Pallas kernels, body(): pl.pallas_call(functools.partial(kernel, heads), out_shape=jax.ShapeDtype...  195 us
    transpose x1, local copies, waits for them, and re-layouts, body(): return jnp.swapaxes(columns, 0, 1)  6.9 us
    unnamed x1, local copies, waits for them, and re-layouts  5.28 us

profile of v1, /device:TPU:0, one launch (start us, length us, event | category | flops | bytes accessed | tf_op | source)
XLA Modules:
  0.0 207.2 jit_solution(5633401006092700904)
XLA Ops:
  0.0 5.3 %copy.11 = bf16[1024,16,128]{2,0,1:T(8,128)(2,1)} copy(bf16[1024,16,128]{2,1,0:T(8,128)(2,1)} %param.7) | data formatting | bytes 8388608 | tf_op args[0]
  5.3 195.0 %shard_map.73 = bf16[128,128,128]{2,1,0:T(8,128)(2,1)} custom-call(bf16[16,1024,128]{2,1,0:T(8,128)(2,1)} %bitcast.5, bf16[2,128,128]{2,1,0:T(8,128)(2,1)} %points_ref.1, bf16[2,2,4,128,128]{4,3,2,1,0:T(8,128)(2,1)} %proj_ref.1, bf16[2,2,128,256]{3,2,1,0:T(8,128)(2,1)} %up_ref.1, bf16[2,2,256,128]{3,2,1,0:T(8,128)(2,1)} %down_ref.1, f32[2,4,128]{2,1,0:T(4,128)} %gain_ref.1, ...), custom_call_target="tpu_custom_call" | custom-call | tf_op jit(solution)/shard_map/pallas_call | solution.py:300
  200.3 6.9 %copy.9 = bf16[128,128,128]{2,1,0:T(8,128)(2,1)} copy(bf16[128,128,128]{2,0,1:T(8,128)(2,1)} %bitcast.4) | data formatting | bytes 8388608 | tf_op jit(solution)/shard_map/transpose | solution.py:335

commit v2 on v1

v2 whole, which is shorter than its diff:
```python
import functools
import math

import jax
import jax.numpy as jnp
from jax import lax
from jax.experimental import pallas as pl
from jax.experimental.pallas import tpu as pltpu
from jax.sharding import PartitionSpec as P

CHUNK = 256
MESH = pl.DeviceIdType.MESH
F32, BF16 = jnp.float32, jnp.bfloat16


def dot(a, b):
    return jnp.dot(a, b, preferred_element_type=F32)


def dot_nt(a, b):
    return lax.dot_general(a, b, (((1,), (1,)), ((), ())), preferred_element_type=F32)


def dot_tn(a, b):
    return lax.dot_general(a, b, (((0,), (0,)), ((), ())), preferred_element_type=F32)


def layer_norm(values, gain_row):
    center = values - jnp.mean(values, axis=-1, keepdims=True)
    spread = jnp.mean(center * center, axis=-1, keepdims=True)
    return (center * lax.rsqrt(spread + 1e-05) * gain_row).astype(BF16)


def unit_rms(values):
    return values * lax.rsqrt(jnp.mean(values * values, axis=-1, keepdims=True) + 1e-06)


def gelu(x):
    c = math.sqrt(2.0 / math.pi)
    return (0.5 * x) * (1.0 + jnp.tanh(x * (c + (c * 0.044715) * (x * x))))


def interleave(chains):
    chains = list(chains)
    while chains:
        for chain in list(chains):
            try:
                next(chain)
            except StopIteration:
                chains.remove(chain)


def kernel(
    heads,
    x_ref,
    points_ref,
    proj_ref,
    up_ref,
    down_ref,
    gain_ref,
    sharp_ref,
    out_ref,
    state,
    final,
    queries,
    probes,
    wkvq,
    wkv2,
    scales,
    sums,
    keys_bd,
    values_bd,
    part,
    row_send,
    row_recv,
    out_send,
    out_recv,
    own_sem,
):
    layers = points_ref.shape[0]
    m, e = points_ref.shape[1], points_ref.shape[2]
    cols, rows = x_ref.shape[0], x_ref.shape[1]
    nrow, nfeat = part.shape[2], out_recv.shape[1]
    block = rows // nfeat
    width = e // heads
    chunks = rows // CHUNK
    slab = m // chunks
    me_r, me_f = lax.axis_index("row"), lax.axis_index("feat")

    def row_peer(d):
        return (lax.rem(me_r + d, nrow), me_f)

    def feat_peer(d):
        return (me_r, lax.rem(me_f + d, nfeat))

    barrier = pltpu.get_barrier_semaphore()
    for d in range(1, nrow):
        pl.semaphore_signal(barrier, inc=1, device_id=row_peer(d), device_id_type=MESH)
    for d in range(1, nfeat):
        pl.semaphore_signal(barrier, inc=1, device_id=feat_peer(d), device_id_type=MESH)

    def head_mask(h, shape):
        return lax.broadcasted_iota(jnp.int32, shape, 1) // width == h

    def lane_scale(b, side):
        scale = jnp.zeros((1, e), F32)
        for h in range(heads):
            scale = jnp.where(head_mask(h, (1, e)), sharp_ref[b, side, h], scale)
        return scale * (math.log2(math.e) / width)

    for b in range(layers):
        for at, (side, which) in enumerate(((0, 1), (0, 2), (1, 0))):
            wkvq[b, :, at * e : (at + 1) * e] = proj_ref[b, side, which]
        for at, (side, which) in enumerate(((1, 1), (1, 2))):
            wkv2[b, :, at * e : (at + 1) * e] = proj_ref[b, side, which]
        probe = unit_rms(dot(points_ref[b], proj_ref[b, 0, 0])) * lane_scale(b, 0)
        for h in range(heads):
            mask = head_mask(h, (m, e))
            probes[b, h * m : (h + 1) * m, :] = jnp.where(mask, probe, 0.0).astype(BF16)
            for slot in range(2):
                values_bd[b, slot, h * m : (h + 1) * m, e:] = mask.astype(F32).astype(BF16)

    pl.semaphore_wait(barrier, nrow - 1 + nfeat - 1)

    def select_spread():
        row = lax.broadcasted_iota(jnp.int32, (16, e), 0)
        lane = lax.broadcasted_iota(jnp.int32, (16, e), 1)
        select = (lane == row * width).astype(F32).astype(BF16)
        spread = (lane // width == row).astype(F32).astype(BF16)
        return row, select, spread

    def by_head(stacked):
        total = stacked[:m]
        for h in range(1, heads):
            total = jnp.where(head_mask(h, (m, e)), stacked[h * m : (h + 1) * m], total)
        return total

    def partial_steps(b, c, at, current):
        normed = layer_norm(current, gain_ref[b, 0][None, :])
        yield
        mixed = dot(normed, wkvq[b])
        values = mixed[:, e : 2 * e].astype(BF16)
        values = jnp.concatenate([values, jnp.ones((CHUNK, e), BF16)], axis=1)
        yield
        keys = unit_rms(mixed[:, :e]).astype(BF16)
        yield
        queries[c, pl.ds(at, CHUNK), :] = unit_rms(mixed[:, 2 * e :]).astype(BF16)
        yield
        weights = jnp.exp2(dot_nt(probes[b], keys)).astype(BF16)
        yield
        stacked = dot(weights, values)
        yield
        sums[b, 0] += by_head(stacked[:, :e])
        sums[b, 1] += by_head(stacked[:, e:])

    def row_steps(b, c, at, current, result):
        slot = lax.rem(c, 2)
        query = queries[c, pl.ds(at, CHUNK), :]
        half = heads * m // 2
        weights = []
        for k in range(2):
            logits = dot_nt(query, keys_bd[b, slot, k * half : (k + 1) * half])
            weights.append(jnp.exp2(logits).astype(BF16))
            yield
        both = dot(jnp.concatenate(weights, axis=1), values_bd[b, slot])
        yield
        attended = (both[:, :e] * pl.reciprocal(both[:, e:], approx=True)).astype(BF16)
        yield
        updated = current + dot(attended, proj_ref[b, 1, 3])
        yield
        normed = layer_norm(updated, gain_ref[b, 3][None, :])
        yield
        hidden = gelu(dot(normed, up_ref[b, 1])).astype(BF16)
        yield
        result.append((updated + dot(hidden, down_ref[b, 1])).astype(BF16))

    def chunk_steps(b, c, at):
        source = x_ref if b <= 1 else state
        current = source[c, pl.ds(at, CHUNK), :].astype(F32)
        if b > 0:
            result = []
            yield from row_steps(b - 1, c, at, current, result)
            if b == layers:
                final[c, pl.ds(at, CHUNK), :] = result[0]
                return
            state[c, pl.ds(at, CHUNK), :] = result[0]
            current = result[0].astype(F32)
            yield
        yield from partial_steps(b, c, at, current)

    def row_copy(b, c, d):
        return pltpu.make_async_remote_copy(
            src_ref=part.at[b, c, 0],
            dst_ref=part.at[b, c, d],
            send_sem=row_send.at[b, c, d],
            recv_sem=row_recv.at[b, c, d],
            device_id=row_peer(d),
            device_id_type=MESH,
        )

    def finish_steps(b, c, i):
        slot = lax.rem(c, 2)
        first = pl.multiple_of(i * slab, slab)
        row, _, spread = select_spread()
        total = part[b, c, 0, m:, :].astype(F32)
        for d in range(1, nrow):
            total = total + part[b, c, d, m:, :].astype(F32)
        inverse = 1.0 / jnp.where(row < heads, total, 1.0)
        high = inverse.astype(BF16)
        low = (inverse - high.astype(F32)).astype(BF16)
        yield
        scales[b] = dot_tn(high, spread) + dot_tn(low, spread)
        yield
        total = part[b, c, 0, pl.ds(first, slab), :].astype(F32)
        for d in range(1, nrow):
            total = total + part[b, c, d, pl.ds(first, slab), :].astype(F32)
        blended = (total * scales[b, pl.ds(first, slab), :]).astype(BF16)
        yield
        anchor = points_ref[b, pl.ds(first, slab), :].astype(F32)
        summary = anchor + dot(blended, proj_ref[b, 0, 3])
        yield
        normed = layer_norm(summary, gain_ref[b, 2][None, :])
        yield
        hidden = gelu(dot(normed, up_ref[b, 0])).astype(BF16)
        yield
        refined = summary + dot(hidden, down_ref[b, 0])
        yield
        normed = layer_norm(refined, gain_ref[b, 1][None, :])
        yield
        mixed = dot(normed, wkv2[b])
        yield
        keys = unit_rms(mixed[:, :e]) * lane_scale(b, 1)
        values = mixed[:, e:]
        for h in range(heads):
            mask = head_mask(h, (slab, e))
            at = pl.ds(pl.multiple_of(h * m + i * slab, slab), slab)
            keys_bd[b, slot, at, :] = jnp.where(mask, keys, 0.0).astype(BF16)
            values_bd[b, slot, at, :e] = jnp.where(mask, values, 0.0).astype(BF16)

    def out_copy(c, d):
        k = lax.rem(me_f + d, nfeat)
        return pltpu.make_async_remote_copy(
            src_ref=final.at[c, pl.ds(k * block, block)],
            dst_ref=out_ref.at[me_f * cols + c],
            send_sem=out_send.at[c, d],
            recv_sem=out_recv.at[c, d],
            device_id=feat_peer(d),
            device_id_type=MESH,
        )

    def own_copy(c):
        return pltpu.make_async_copy(
            final.at[c, pl.ds(me_f * block, block)],
            out_ref.at[me_f * cols + c],
            own_sem.at[c],
        )

    jobs = []
    for b in range(layers + 1):
        jobs.append((3 * b, "stage", b))
        if b < layers:
            jobs.append((3 * b + 2, "finish", b))

    def turn(active, s):
        for lag, kind, b in active:
            if kind == "finish":
                for d in range(1, nrow):
                    copy = row_copy(b, s - lag, d)
                    copy.wait_send()
                    copy.wait_recv()
            elif b < layers:
                sums[b] = jnp.zeros((2, m, e), F32)

        def step(i, carry):
            at = pl.multiple_of(i * CHUNK, CHUNK)
            interleave(
                chunk_steps(b, s - lag, at) if kind == "stage" else finish_steps(b, s - lag, i)
                for lag, kind, b in active
            )
            return carry

        lax.fori_loop(0, chunks, step, 0)
        for lag, kind, b in active:
            c = s - lag
            if kind == "finish":
                continue
            if b < layers:
                _, select, _ = select_spread()
                part[b, c, 0, :m, :] = sums[b, 0].astype(BF16)
                part[b, c, 0, m:, :] = dot_nt(select, sums[b, 1].astype(BF16)).astype(BF16)
                for d in range(1, nrow):
                    row_copy(b, c, d).start()
            else:
                for d in range(1, nfeat):
                    out_copy(c, d).start()
                own_copy(c).start()

    turns = [
        tuple(job for job in jobs if 0 <= s - job[0] < cols) for s in range(cols + 3 * layers)
    ]
    s = 0
    while s < len(turns):
        end = s
        while end < len(turns) and turns[end] == turns[s]:
            end += 1
        active = turns[s]

        def run(at, carry, active=active):
            turn(active, at)
            return carry

        lax.fori_loop(s, end, run, 0)
        s = end

    def drain(c, carry):
        for d in range(1, nfeat):
            out_copy(c, d).wait_send()
            source = lax.rem(me_f + nfeat - d, nfeat)
            pltpu.make_async_remote_copy(
                src_ref=final.at[c, pl.ds(me_f * block, block)],
                dst_ref=out_ref.at[source * cols + c],
                send_sem=out_send.at[c, d],
                recv_sem=out_recv.at[c, d],
                device_id=feat_peer(d),
                device_id_type=MESH,
            ).wait_recv()
        own_copy(c).wait()
        return carry

    lax.fori_loop(0, cols, drain, 0)


def body(
    table_entries,
    pseudo_points,
    projection_tensors,
    expanding_linear,
    contracting_linear,
    normalizer_multipliers,
    sharpness_coefficients,
    *,
    nrow,
    nfeat,
):
    rows, cols, e = table_entries.shape
    layers, m = pseudo_points.shape[:2]
    heads = sharpness_coefficients.shape[2]
    vmem = pl.BlockSpec(memory_space=pltpu.VMEM)
    columns = pl.pallas_call(
        functools.partial(kernel, heads),
        out_shape=jax.ShapeDtypeStruct((cols * nfeat, rows // nfeat, e), BF16),
        in_specs=[vmem] * 6 + [pl.BlockSpec(memory_space=pltpu.SMEM)],
        out_specs=pl.BlockSpec(memory_space=pl.ANY),
        scratch_shapes=[
            pltpu.VMEM((cols, rows, e), BF16),
            pltpu.VMEM((cols, rows, e), BF16),
            pltpu.VMEM((cols, rows, e), BF16),
            pltpu.VMEM((layers, heads * m, e), BF16),
            pltpu.VMEM((layers, e, 3 * e), BF16),
            pltpu.VMEM((layers, e, 2 * e), BF16),
            pltpu.VMEM((layers, m, e), F32),
            pltpu.VMEM((layers, 2, m, e), F32),
            pltpu.VMEM((layers, 2, heads * m, e), BF16),
            pltpu.VMEM((layers, 2, heads * m, 2 * e), BF16),
            pltpu.VMEM((layers, cols, nrow, m + 16, e), BF16),
            pltpu.SemaphoreType.DMA((layers, cols, nrow)),
            pltpu.SemaphoreType.DMA((layers, cols, nrow)),
            pltpu.SemaphoreType.DMA((cols, nfeat)),
            pltpu.SemaphoreType.DMA((cols, nfeat)),
            pltpu.SemaphoreType.DMA((cols,)),
        ],
        compiler_params=pltpu.CompilerParams(
            collective_id=0, has_side_effects=True, vmem_limit_bytes=56 * 2**20
        ),
    )(
        jnp.swapaxes(table_entries, 0, 1),
        pseudo_points,
        projection_tensors,
        expanding_linear,
        contracting_linear,
        normalizer_multipliers,
        sharpness_coefficients,
    )
    return jnp.swapaxes(columns, 0, 1)


def solution(mesh):
    return jax.shard_map(
        functools.partial(body, nrow=mesh.shape["row"], nfeat=mesh.shape["feat"]),
        mesh=mesh,
        in_specs=(P("row", "feat", None), P(), P(), P(), P(), P(), P()),
        out_specs=P(("row", "feat"), None, None),
        check_vma=False,
    )
```

time: 209 us -> 197 us (0.943)
  Pallas kernels: 195 us -> 184 us
    pallas_call x1, Pallas kernels: 195 us -> 184 us  [body(): pl.pallas_call(functools.partial(kernel, heads), out_shape=jax.ShapeDtype...]
where the time goes in v2:
time: 197 us
  Pallas kernels  184 us (93%)
  local copies, waits for them, and re-layouts  12.2 us (6%)
    pallas_call x1, Pallas kernels, body(): pl.pallas_call(functools.partial(kernel, heads), out_shape=jax.ShapeDtype...  184 us
    transpose x1, local copies, waits for them, and re-layouts, body(): return jnp.swapaxes(columns, 0, 1)  6.9 us
    unnamed x1, local copies, waits for them, and re-layouts  5.28 us

profile of v2, /device:TPU:0, one launch (start us, length us, event | category | flops | bytes accessed | tf_op | source)
XLA Modules:
  0.0 196.5 jit_solution(14796277189967760249)
XLA Ops:
  0.0 5.3 %copy.11 = bf16[1024,16,128]{2,0,1:T(8,128)(2,1)} copy(bf16[1024,16,128]{2,1,0:T(8,128)(2,1)} %param.7) | data formatting | bytes 8388608 | tf_op args[0]
  5.3 184.3 %shard_map.73 = bf16[128,128,128]{2,1,0:T(8,128)(2,1)} custom-call(bf16[16,1024,128]{2,1,0:T(8,128)(2,1)} %bitcast.5, bf16[2,128,128]{2,1,0:T(8,128)(2,1)} %points_ref.1, bf16[2,2,4,128,128]{4,3,2,1,0:T(8,128)(2,1)} %proj_ref.1, bf16[2,2,128,256]{3,2,1,0:T(8,128)(2,1)} %up_ref.1, bf16[2,2,256,128]{3,2,1,0:T(8,128)(2,1)} %down_ref.1, f32[2,4,128]{2,1,0:T(4,128)} %gain_ref.1, ...), custom_call_target="tpu_custom_call" | custom-call | tf_op jit(solution)/shard_map/pallas_call | solution.py:349
  189.6 6.9 %copy.9 = bf16[128,128,128]{2,1,0:T(8,128)(2,1)} copy(bf16[128,128,128]{2,0,1:T(8,128)(2,1)} %bitcast.4) | data formatting | bytes 8388608 | tf_op jit(solution)/shard_map/transpose | solution.py:384

commit v3 on v2

--- a/solution.py
+++ b/solution.py
@@ -8,7 +8,7 @@
 from jax.experimental.pallas import tpu as pltpu
 from jax.sharding import PartitionSpec as P
 
-CHUNK = 256
+CHUNK = 512
 MESH = pl.DeviceIdType.MESH
 F32, BF16 = jnp.float32, jnp.bfloat16
 
@@ -37,7 +37,9 @@
 
 def gelu(x):
     c = math.sqrt(2.0 / math.pi)
-    return (0.5 * x) * (1.0 + jnp.tanh(x * (c + (c * 0.044715) * (x * x))))
+    x = x.astype(BF16)
+    half = BF16(0.5) * x
+    return half + half * jnp.tanh(x * (BF16(c) + BF16(c * 0.044715) * (x * x)))
 
 
 def interleave(chains):
@@ -146,7 +148,7 @@
         yield
         queries[c, pl.ds(at, CHUNK), :] = unit_rms(mixed[:, 2 * e :]).astype(BF16)
         yield
-        weights = jnp.exp2(dot_nt(probes[b], keys)).astype(BF16)
+        weights = jnp.exp2(dot_nt(probes[b], keys).astype(BF16))
         yield
         stacked = dot(weights, values)
         yield
@@ -160,7 +162,7 @@
         weights = []
         for k in range(2):
             logits = dot_nt(query, keys_bd[b, slot, k * half : (k + 1) * half])
-            weights.append(jnp.exp2(logits).astype(BF16))
+            weights.append(jnp.exp2(logits.astype(BF16)))
             yield
         both = dot(jnp.concatenate(weights, axis=1), values_bd[b, slot])
         yield
@@ -170,7 +172,7 @@
         yield
         normed = layer_norm(updated, gain_ref[b, 3][None, :])
         yield
-        hidden = gelu(dot(normed, up_ref[b, 1])).astype(BF16)
+        hidden = gelu(dot(normed, up_ref[b, 1]))
         yield
         result.append((updated + dot(hidden, down_ref[b, 1])).astype(BF16))
 
@@ -221,7 +223,7 @@
         yield
         normed = layer_norm(summary, gain_ref[b, 2][None, :])
         yield
-        hidden = gelu(dot(normed, up_ref[b, 0])).astype(BF16)
+        hidden = gelu(dot(normed, up_ref[b, 0]))
         yield
         refined = summary + dot(hidden, down_ref[b, 0])
         yield

time: 197 us -> 155 us (0.79)
  Pallas kernels: 184 us -> 143 us
    pallas_call x1, Pallas kernels: 184 us -> 143 us  [body(): pl.pallas_call(functools.partial(kernel, heads), out_shape=jax.ShapeDtype...]
where the time goes in v3:
time: 155 us
  Pallas kernels  143 us (92%)
  local copies, waits for them, and re-layouts  12.2 us (8%)
    pallas_call x1, Pallas kernels, body(): pl.pallas_call(functools.partial(kernel, heads), out_shape=jax.ShapeDtype...  143 us
    transpose x1, local copies, waits for them, and re-layouts, body(): return jnp.swapaxes(columns, 0, 1)  6.9 us
    unnamed x1, local copies, waits for them, and re-layouts  5.28 us

profile of v3, /device:TPU:0, one launch (start us, length us, event | category | flops | bytes accessed | tf_op | source)
XLA Modules:
  0.0 155.2 jit_solution(3940127379276269062)
XLA Ops:
  0.0 5.3 %copy.11 = bf16[1024,16,128]{2,0,1:T(8,128)(2,1)} copy(bf16[1024,16,128]{2,1,0:T(8,128)(2,1)} %param.7) | data formatting | bytes 8388608 | tf_op args[0]
  5.3 143.0 %shard_map.73 = bf16[128,128,128]{2,1,0:T(8,128)(2,1)} custom-call(bf16[16,1024,128]{2,1,0:T(8,128)(2,1)} %bitcast.5, bf16[2,128,128]{2,1,0:T(8,128)(2,1)} %points_ref.1, bf16[2,2,4,128,128]{4,3,2,1,0:T(8,128)(2,1)} %proj_ref.1, bf16[2,2,128,256]{3,2,1,0:T(8,128)(2,1)} %up_ref.1, bf16[2,2,256,128]{3,2,1,0:T(8,128)(2,1)} %down_ref.1, f32[2,4,128]{2,1,0:T(4,128)} %gain_ref.1, ...), custom_call_target="tpu_custom_call" | custom-call | tf_op jit(solution)/shard_map/pallas_call | solution.py:351
  148.3 6.9 %copy.9 = bf16[128,128,128]{2,1,0:T(8,128)(2,1)} copy(bf16[128,128,128]{2,0,1:T(8,128)(2,1)} %bitcast.4) | data formatting | bytes 8388608 | tf_op jit(solution)/shard_map/transpose | solution.py:386

commit v4 on v3

--- a/solution.py
+++ b/solution.py
@@ -35,11 +35,22 @@
     return values * lax.rsqrt(jnp.mean(values * values, axis=-1, keepdims=True) + 1e-06)
 
 
-def gelu(x):
+def bare_norm(values):
+    e = values.shape[-1]
+    center = values - jnp.mean(values, axis=-1, keepdims=True)
+    total = jnp.sum(center * center, axis=-1, keepdims=True)
+    return (center * lax.rsqrt(total + e * 1e-05)).astype(BF16)
+
+
+def bare_rms(values):
+    total = jnp.sum(values * values, axis=-1, keepdims=True)
+    return (values * lax.rsqrt(total + values.shape[-1] * 1e-06)).astype(BF16)
+
+
+def gelu2(x):
     c = math.sqrt(2.0 / math.pi)
     x = x.astype(BF16)
-    half = BF16(0.5) * x
-    return half + half * jnp.tanh(x * (BF16(c) + BF16(c * 0.044715) * (x * x)))
+    return x + x * jnp.tanh(x * (BF16(c) + BF16(c * 0.044715) * (x * x)))
 
 
 def interleave(chains):
@@ -68,6 +79,8 @@
     probes,
     wkvq,
     wkv2,
+    up_row,
+    down_half,
     scales,
     sums,
     keys_bd,
@@ -108,11 +121,21 @@
         scale = jnp.zeros((1, e), F32)
         for h in range(heads):
             scale = jnp.where(head_mask(h, (1, e)), sharp_ref[b, side, h], scale)
-        return scale * (math.log2(math.e) / width)
+        return scale * (math.sqrt(e) * math.log2(math.e) / width)
+
+    def with_gain(gain, weight):
+        eye = lax.broadcasted_iota(jnp.int32, (e, e), 0) == lax.broadcasted_iota(
+            jnp.int32, (e, e), 1
+        )
+        column = jnp.sum(jnp.where(eye, gain[None, :], 0.0), axis=1, keepdims=True)
+        return (weight.astype(F32) * (column * math.sqrt(e))).astype(BF16)
 
     for b in range(layers):
         for at, (side, which) in enumerate(((0, 1), (0, 2), (1, 0))):
-            wkvq[b, :, at * e : (at + 1) * e] = proj_ref[b, side, which]
+            wkvq[b, :, at * e : (at + 1) * e] = with_gain(gain_ref[b, 0], proj_ref[b, side, which])
+        up_row[b] = with_gain(gain_ref[b, 3], up_ref[b, 1])
+        for side in range(2):
+            down_half[b, side] = (down_ref[b, side].astype(F32) * 0.5).astype(BF16)
         for at, (side, which) in enumerate(((1, 1), (1, 2))):
             wkv2[b, :, at * e : (at + 1) * e] = proj_ref[b, side, which]
         probe = unit_rms(dot(points_ref[b], proj_ref[b, 0, 0])) * lane_scale(b, 0)
@@ -138,15 +161,15 @@
         return total
 
     def partial_steps(b, c, at, current):
-        normed = layer_norm(current, gain_ref[b, 0][None, :])
+        normed = bare_norm(current)
         yield
         mixed = dot(normed, wkvq[b])
         values = mixed[:, e : 2 * e].astype(BF16)
         values = jnp.concatenate([values, jnp.ones((CHUNK, e), BF16)], axis=1)
         yield
-        keys = unit_rms(mixed[:, :e]).astype(BF16)
-        yield
-        queries[c, pl.ds(at, CHUNK), :] = unit_rms(mixed[:, 2 * e :]).astype(BF16)
+        keys = bare_rms(mixed[:, :e])
+        yield
+        queries[c, pl.ds(at, CHUNK), :] = bare_rms(mixed[:, 2 * e :])
         yield
         weights = jnp.exp2(dot_nt(probes[b], keys).astype(BF16))
         yield
@@ -170,11 +193,11 @@
         yield
         updated = current + dot(attended, proj_ref[b, 1, 3])
         yield
-        normed = layer_norm(updated, gain_ref[b, 3][None, :])
-        yield
-        hidden = gelu(dot(normed, up_ref[b, 1]))
-        yield
-        result.append((updated + dot(hidden, down_ref[b, 1])).astype(BF16))
+        normed = bare_norm(updated)
+        yield
+        hidden = gelu2(dot(normed, up_row[b]))
+        yield
+        result.append((updated + dot(hidden, down_half[b, 1])).astype(BF16))
 
     def chunk_steps(b, c, at):
         source = x_ref if b <= 1 else state
@@ -223,9 +246,9 @@
         yield
         normed = layer_norm(summary, gain_ref[b, 2][None, :])
         yield
-        hidden = gelu(dot(normed, up_ref[b, 0]))
-        yield
-        refined = summary + dot(hidden, down_ref[b, 0])
+        hidden = gelu2(dot(normed, up_ref[b, 0]))
+        yield
+        refined = summary + dot(hidden, down_half[b, 0])
         yield
         normed = layer_norm(refined, gain_ref[b, 1][None, :])
         yield
@@ -360,6 +383,8 @@
             pltpu.VMEM((layers, heads * m, e), BF16),
             pltpu.VMEM((layers, e, 3 * e), BF16),
             pltpu.VMEM((layers, e, 2 * e), BF16),
+            pltpu.VMEM((layers,) + expanding_linear.shape[2:], BF16),
+            pltpu.VMEM(contracting_linear.shape, BF16),
             pltpu.VMEM((layers, m, e), F32),
             pltpu.VMEM((layers, 2, m, e), F32),
             pltpu.VMEM((layers, 2, heads * m, e), BF16),

time: 155 us -> 155 us (level)
  no operation moved by 1% of the time
where the time goes in v4:
time: 155 us
  Pallas kernels  142 us (92%)
  local copies, waits for them, and re-layouts  12.2 us (8%)
    pallas_call x1, Pallas kernels, body(): pl.pallas_call(functools.partial(kernel, heads), out_shape=jax.ShapeDtype...  142 us
    transpose x1, local copies, waits for them, and re-layouts, body(): return jnp.swapaxes(columns, 0, 1)  6.9 us
    unnamed x1, local copies, waits for them, and re-layouts  5.28 us

profile of v4, /device:TPU:0, one launch (start us, length us, event | category | flops | bytes accessed | tf_op | source)
XLA Modules:
  0.0 154.6 jit_solution(8579700294885307001)
XLA Ops:
  0.0 5.3 %copy.11 = bf16[1024,16,128]{2,0,1:T(8,128)(2,1)} copy(bf16[1024,16,128]{2,1,0:T(8,128)(2,1)} %param.7) | data formatting | bytes 8388608 | tf_op args[0]
  5.3 142.4 %shard_map.73 = bf16[128,128,128]{2,1,0:T(8,128)(2,1)} custom-call(bf16[16,1024,128]{2,1,0:T(8,128)(2,1)} %bitcast.5, bf16[2,128,128]{2,1,0:T(8,128)(2,1)} %points_ref.1, bf16[2,2,4,128,128]{4,3,2,1,0:T(8,128)(2,1)} %proj_ref.1, bf16[2,2,128,256]{3,2,1,0:T(8,128)(2,1)} %up_ref.1, bf16[2,2,256,128]{3,2,1,0:T(8,128)(2,1)} %down_ref.1, f32[2,4,128]{2,1,0:T(4,128)} %gain_ref.1, ...), custom_call_target="tpu_custom_call" | custom-call | tf_op jit(solution)/shard_map/pallas_call | solution.py:374
  147.7 6.9 %copy.9 = bf16[128,128,128]{2,1,0:T(8,128)(2,1)} copy(bf16[128,128,128]{2,0,1:T(8,128)(2,1)} %bitcast.4) | data formatting | bytes 8388608 | tf_op jit(solution)/shard_map/transpose | solution.py:411
